TPU v7x, 128 devices: a whole 4x4x4 slice. The times are simulated.
128 devices in a mesh: row: 4 (over x), col: 8 (over z, core), depth: 4 (over y).
Axes of the slice: x: 4, y: 4, z: 4, core: 2. Of those that a mesh axis runs over, the one named last changes fastest.
Arguments:
- policy_states: bfloat16 [1024, 5120], P(('col', 'depth'), 'row'), may hold values from -40 to 40
- reference_states: bfloat16 [1024, 5120], P(('row', 'col', 'depth')), may hold values from -40 to 40
- policy_weight: bfloat16 [5120, 81920], P('row', ('col', 'depth'))
- reference_weight: bfloat16 [5120, 81920], P(None, ('row', 'col', 'depth'))
- targets: int32 [1024], replicated, may hold values from 0 to 81919
- response_mask: int32 [1024], replicated, may hold values from 0 to 1, as said below
- pair_index: int32 [8], replicated, may hold values from 0 to 3, as said below
- chosen_flag: int32 [8], replicated, may hold values from 0 to 1, as said below
Outputs:
- loss: float32 [], replicated
- grad_states: float32 [1024, 5120], P(('col', 'depth'), 'row')
- grad_weight: float32 [5120, 81920], P('row', ('col', 'depth'))
Inputs may be any that keep to these rules, and one draw needn't show every extreme that they name: `response_mask`: in each sequence of 128 tokens the ones form one run of at least 32 tokens that begins at or after position 16. `pair_index`: each pair names exactly two sequences. `chosen_flag`: the two sequences of a pair have flags 1 and 0.
All inputs are finite; a program needn't handle non-finite values.
Results may differ from a plain program's by a relative error of at most 0.0022.
Values may be sent and summed in bfloat16 or wider, within the bound.
A program may use at most 128 MiB of HBM per device.

v0:
```python
import functools

import jax
import jax.numpy as jnp
from jax import lax
from jax.experimental import pallas as pl
from jax.experimental.pallas import tpu as pltpu
from jax.sharding import PartitionSpec as P

PAIRS = 4
LEN = 128
SEQS = 8
SKIP = 16
KEEP = LEN - SKIP
SIZES = (176, 2 * KEEP)

beta_value = 0.1
loss_scale = 256.0

MESH = pl.DeviceIdType.MESH
VMEM_LIMIT = 62 * 1024 * 1024
ROWS = 16


def preference(ratio, pair_index, chosen_flag):
    sign = (2 * chosen_flag - 1).astype(jnp.float32)
    member = pair_index[:, None] == jnp.arange(PAIRS, dtype=jnp.int32)[None, :]
    margin = jnp.sum(jnp.where(member, (sign * ratio)[:, None], 0.0), axis=0)
    loss = -jnp.mean(jax.nn.log_sigmoid(beta_value * margin))
    slope = -loss_scale * beta_value / PAIRS * jax.nn.sigmoid(-beta_value * margin)
    weights = sign * jnp.sum(jnp.where(member, slope[None, :], 0.0), axis=1)
    return (loss, weights)


class Place:
    def __init__(self):
        self.x = lax.axis_index("row")
        col = lax.axis_index("col")
        self.z = col // 2
        self.c = col % 2
        self.y = lax.axis_index("depth")

    def on_x(self, step):
        return ((self.x + step) % 4, self.z * 2 + self.c, self.y)

    def on_y(self, step):
        return (self.x, self.z * 2 + self.c, (self.y + step) % 4)

    def on_z(self, step):
        return (self.x, ((self.z + step) % 4) * 2 + self.c, self.y)

    def partner_y(self):
        return (self.x, self.z * 2 + self.c, self.y + 1 - 2 * (self.y % 2))

    def other_core(self):
        return (self.x, self.z * 2 + 1 - self.c, self.y)


def greet(peers):
    barrier = pltpu.get_barrier_semaphore()
    for peer in peers:
        pl.semaphore_signal(barrier, inc=1, device_id=peer, device_id_type=MESH)
    pl.semaphore_wait(barrier, len(peers))


class Mover:
    def __init__(self, send, recv):
        self.send, self.recv, self.used, self.all = send, recv, 0, []

    def make(self, k, src, dst, peer):
        return pltpu.make_async_remote_copy(
            src_ref=src,
            dst_ref=dst,
            send_sem=self.send.at[k],
            recv_sem=self.recv.at[k],
            device_id=peer,
            device_id_type=MESH,
        )

    def start(self, src, dst, peer):
        copy = self.make(self.used, src, dst, peer)
        self.used += 1
        copy.start()
        self.all.append(copy)
        return copy

    def sent(self, copy):
        copy.wait_send()
        self.all = [other for other in self.all if other is not copy]

    def finish(self):
        for copy in self.all:
            copy.wait_send()


class Ring:
    def __init__(self, mover, me, view, peer):
        self.mover, self.me, self.view, self.peer = mover, me, view, peer

    def begin(self):
        own = self.view(self.me, None)
        self.right = self.mover.start(own, own, self.peer(1))
        self.left = self.mover.start(own, own, self.peer(3))

    def forward(self):
        self.right.wait_recv()
        part = self.view((self.me + 3) % 4, 0)
        self.far_right = self.mover.start(part, part, self.peer(1))
        self.left.wait_recv()
        part = self.view((self.me + 1) % 4, 1)
        self.far_left = self.mover.start(part, part, self.peer(3))

    def end(self):
        self.far_right.wait_recv()
        self.far_left.wait_recv()


def merge(a, b):
    peak = jnp.maximum(a[..., 0:1, :], b[..., 0:1, :])
    total = a[..., 1:2, :] * jnp.exp(a[..., 0:1, :] - peak) + b[..., 1:2, :] * jnp.exp(
        b[..., 0:1, :] - peak
    )
    return jnp.concatenate([peak, total, a[..., 2:3, :] + b[..., 2:3, :], a[..., 3:, :]], axis=-2)


def over(count, read, write, unroll):
    def group(steps):
        rows = [pl.ds(pl.multiple_of(step * ROWS, ROWS), ROWS) for step in steps]
        for r, value in zip(rows, [read(r) for r in rows]):
            write(r, value)

    steps = count // ROWS
    whole = steps // unroll

    @pl.loop(0, whole)
    def _(g):
        group([g * unroll + u for u in range(unroll)])

    if steps % unroll:
        group(list(range(whole * unroll, steps)))


def wide(value, width):
    return jnp.concatenate([value] * (width // 128), axis=1)


def fold(op, value):
    parts = [value[:, k : k + 128] for k in range(0, value.shape[1], 128)]
    while len(parts) > 1:
        paired = [op(a, b) for a, b in zip(parts[::2], parts[1::2])]
        parts = paired + parts[len(paired) * 2 :]
    return parts[0]


def to_column(row):
    return jnp.transpose(jnp.broadcast_to(row, (128, row.shape[1])))


def span(half, count):
    return slice(None) if half is None else pl.ds(half * (count // 2), count // 2)


def fused_kernel(
    own,
    ref_own,
    weight_in,
    ref_weight_in,
    masks,
    wanted,
    pairs,
    loss,
    rows_out,
    grad_out,
    kept,
    weight,
    ref_weight,
    gathered,
    ref_half,
    ref_got,
    refs,
    partial,
    qsend,
    qrecv,
    ssend,
    srecv,
    column,
    inverse,
    third,
    kept_wanted,
    choose,
    place,
    kept_mask,
    spread,
    ref_logits,
    ref_column,
    ref_wanted,
    ref_stats,
    ref_first,
    held,
    got,
    info,
    token_weights,
    grad,
    grad_full,
    rows_all,
    core_send,
    core_recv,
    y_send,
    y_recv,
    z_send,
    z_recv,
    z_sum,
    row_ssend,
    row_srecv,
    send,
    recv,
    local,
):
    at = Place()
    x, z, c, y = at.x, at.z, at.c, at.y
    share, width = spread.shape[1], spread.shape[2]
    depth = own.shape[1]
    half = width // 2
    f32, bf16 = jnp.float32, jnp.bfloat16
    fetch = [
        pltpu.make_async_copy(weight_in, weight, local.at[4]),
        pltpu.make_async_copy(ref_weight_in, ref_weight, local.at[5]),
    ]
    for copy in fetch:
        copy.start()
    ways = [at.on_x, at.on_y, at.on_z]
    greet([way(i) for way in ways for i in (1, 2, 3)] + [at.other_core()])
    move = Mover(send, recv)

    gathered[z, c, y] = own[...]
    low, high = pl.ds(0, depth // 2), pl.ds(depth // 2, depth // 2)
    count = own.shape[0]
    first_y = Ring(move, y, lambda i, h: gathered.at[z, c, i, span(h, count), low], at.on_y)
    first_z = Ring(move, z, lambda i, h: gathered.at[i, c, y, span(h, count), high], at.on_z)
    then_z = Ring(move, z, lambda i, h: gathered.at[i, c, span(h, 4), :, low], at.on_z)
    then_y = Ring(move, y, lambda i, h: gathered.at[span(h, 4), c, i, :, high], at.on_y)
    first_y.begin()
    first_z.begin()

    side, pair = y % 2, y // 2
    ref_depth = ref_own.shape[1]
    quarter = ref_depth // 4
    for k in (0, 1):
        ref_half[k] = ref_own[:, k * 2 * quarter : (k + 1) * 2 * quarter].astype(f32)
    swap = move.start(ref_half.at[1 - side], ref_got, at.partner_y())
    column[...] = jnp.zeros_like(column)
    first_y.forward()
    first_z.forward()
    swap.wait_recv()
    mine, theirs = ref_half[side], ref_got[...]
    block = jnp.concatenate(
        [jnp.where(side == 0, mine, theirs), jnp.where(side == 0, theirs, mine)], axis=0
    ).astype(bf16)
    for f in (0, 1):
        refs[x, z, c, f, pair, side] = block[:, f * quarter : (f + 1) * quarter]
    ref_x = Ring(
        move,
        x,
        lambda i, h: refs.at[i, z, c, slice(None) if h is None else h, pair, side],
        at.on_x,
    )
    ref_y = Ring(move, y, lambda i, h: refs.at[span(h, 4), z, c, 0, i // 2, i % 2], at.on_y)
    ref_z = Ring(move, z, lambda i, h: refs.at[span(h, 4), i, c, 1, pair, side], at.on_z)
    ref_yz = Ring(move, z, lambda i, h: refs.at[span(h, 4), i, c, 0], at.on_z)
    ref_zy = Ring(move, y, lambda i, h: refs.at[span(h, 4), :, c, 1, i // 2, i % 2], at.on_y)
    ref_core = []

    def to_core(ring, i):
        part = ring.view((ring.me + i) % 4, None)
        ref_core.append(move.start(part, part, at.other_core()))

    own_core = []

    def share_core(ring, steps):
        for i in steps:
            part = ring.view((ring.me + i) % 4, None)
            own_core.append(move.start(part, part, at.other_core()))

    first_y.end()
    then_z.begin()
    share_core(then_z, (0,))
    first_z.end()
    then_y.begin()
    share_core(then_y, (0,))
    ref_x.begin()

    def runs(owner):
        lane = lax.broadcasted_iota(jnp.int32, (1, 2 * LEN), 1)
        mask = masks[owner]
        a = jnp.where(lane < LEN, mask, 0)
        b = jnp.where(lane < LEN, 0, mask)
        return (
            jnp.sum(a, axis=1, keepdims=True),
            jnp.sum(b, axis=1, keepdims=True),
            jnp.min(jnp.where(a > 0, lane, 2 * LEN), axis=1, keepdims=True),
            jnp.min(jnp.where(b > 0, lane, 2 * LEN), axis=1, keepdims=True),
        )

    def source(owner, i):
        len_a, len_b, start_a, start_b = runs(owner)
        second = jnp.where(i < len_a + len_b, start_b + i - len_a, -1)
        return jnp.where(i < len_a, start_a + i, second)

    def kept_masks(owner):
        len_a, len_b, _, _ = runs(owner)
        i = lax.broadcasted_iota(jnp.int32, (1, 2 * LEN), 1)
        a = (i < len_a).astype(f32)
        return a, (i < len_a + len_b).astype(f32) - a

    for k in range(4):
        ref_wanted[k] = to_column(wanted[k].astype(f32))

    @pl.loop(0, 4)
    def _(o):
        to = source(o, lax.broadcasted_iota(jnp.int32, (share, 1), 0))
        here = lax.broadcasted_iota(jnp.int32, (share, 2 * LEN), 1) == to
        choose[o] = here.astype(bf16)
        target = jnp.sum(jnp.where(here, wanted[o].astype(f32), 0.0), axis=1, keepdims=True)
        kept_wanted[o] = jnp.broadcast_to(target, (share, 128))
        to = source(o, lax.broadcasted_iota(jnp.int32, (1, share), 1))
        place[o] = (lax.broadcasted_iota(jnp.int32, (2 * LEN, share), 0) == to).astype(bf16)
        mask_a, mask_b = kept_masks(o)
        kept_mask[o, 0:1, :] = mask_a
        kept_mask[o, 1:2, :] = mask_b

    then_z.forward()
    share_core(then_z, (1, 3))
    then_y.forward()
    share_core(then_y, (1, 3))
    ref_x.forward()
    then_z.end()
    share_core(then_z, (2,))
    then_y.end()
    share_core(then_y, (2,))
    ref_x.end()
    ref_y.begin()
    ref_z.begin()
    fetch[0].wait()
    for copy in own_core:
        copy.wait_recv()

    tile = 256

    def product(owner):
        whole = gathered[owner].reshape(2 * LEN, depth)
        kept[owner] = jnp.dot(choose[owner], whole, preferred_element_type=f32).astype(bf16)

        @pl.loop(0, width // tile)
        def _(j):
            cols = pl.ds(pl.multiple_of(j * tile, tile), tile)
            partial[owner, :, cols] = jnp.dot(
                kept[owner], weight[:, cols], preferred_element_type=f32
            )

    def encode(count, read, write, store=None):
        def top(rows, value):
            if store is not None:
                store(rows, value)
            column[rows, :] = fold(jnp.maximum, jnp.abs(value))

        over(count, read, top, 2)
        peak = jnp.max(column[0:count, :], axis=1, keepdims=True)
        step = jnp.broadcast_to(jnp.maximum(peak, 1e-30) * (1.0 / 32767.0), (count, 128))
        column[0:count, :] = step
        inverse[0:count, :] = 1.0 / step

        def code(rows):
            value = read(rows) if store is None else store(rows)
            value = value * wide(inverse[rows, :], value.shape[1])
            return jnp.round(value).astype(jnp.int32).astype(jnp.int16)

        over(count, code, write, 2)
        return jnp.transpose(column[...])[0:8]

    def decode(code, step):
        return code.astype(jnp.int32).astype(f32) * wide(step, code.shape[1])

    def pack(k, owner, part, peer, add=None):
        cols = pl.ds(part * half, half)
        slot = k % 3 % 2 + k // 3 * 2

        def plain(rows):
            return partial[owner, rows, cols]

        def summed(rows):
            return plain(rows) + decode(qrecv[add, rows, :], third[rows, :])

        def store(rows, value=None):
            if value is None:
                return plain(rows)
            partial[owner, rows, cols] = value

        def write(rows, code):
            qsend[slot, rows, :] = code

        if add is None:
            ssend[k] = encode(share, plain, write)
        else:
            third[...] = to_column(srecv[add, 0:1, :])
            ssend[k] = encode(share, summed, write, store)
        return (
            move.start(ssend.at[k], srecv.at[k], peer),
            move.start(qsend.at[slot], qrecv.at[k], peer),
        )

    def arrived(copies):
        for copy in copies:
            copy.wait_recv()

    def add_in(k, part):
        cols = pl.ds(part * half, half)
        column[...] = to_column(srecv[k, 0:1, :])

        def read(rows):
            return partial[x, rows, cols] + decode(qrecv[k, rows, :], column[rows, :])

        def write(rows, value):
            partial[x, rows, cols] = value

        over(share, read, write, 2)

    right, left = at.on_x(1), at.on_x(3)
    after, before, across = (x + 1) % 4, (x + 3) % 4, (x + 2) % 4
    product(across)
    r0 = pack(0, across, 0, right)
    l0 = pack(3, across, 1, left)
    ref_y.forward()
    ref_z.forward()
    product(after)
    r1 = pack(1, after, 1, right)
    product(before)
    l1 = pack(4, before, 0, left)
    ref_y.end()
    ref_yz.begin()
    to_core(ref_yz, 0)
    ref_z.end()
    ref_zy.begin()
    to_core(ref_zy, 0)
    product(x)
    arrived(r0)
    move.sent(r0[1])
    r2 = pack(2, after, 0, right, add=0)
    arrived(l0)
    move.sent(l0[1])
    l2 = pack(5, before, 1, left, add=3)
    ref_yz.forward()
    to_core(ref_yz, 1)
    to_core(ref_yz, 3)
    ref_zy.forward()
    to_core(ref_zy, 1)
    to_core(ref_zy, 3)
    arrived(r1)
    add_in(1, 1)
    arrived(l1)
    add_in(4, 0)
    ref_yz.end()
    to_core(ref_yz, 2)
    ref_zy.end()
    to_core(ref_zy, 2)
    arrived(r2)
    arrived(l2)
    column[...] = to_column(srecv[2, 0:1, :])
    third[...] = to_column(srecv[5, 0:1, :])
    first = (lax.axis_index("col") * 4 + y) * width

    def entries(rows_count):
        lane = lax.broadcasted_iota(jnp.int32, (rows_count, width), 1)
        return (lane + first).astype(f32)

    def read(rows):
        codes = (decode(qrecv[2, rows, :], column[rows, :]), decode(qrecv[5, rows, :], third[rows, :]))
        return partial[x, rows, :] + jnp.concatenate(codes, axis=1)

    def write(rows, value):
        partial[x, rows, :] = value
        hits = entries(ROWS) == wide(kept_wanted[x, rows, :], width)
        column[rows, :] = fold(jnp.maximum, value)
        third[rows, :] = fold(jnp.add, jnp.where(hits, value, 0.0))

    over(share, read, write, 1)
    peak = jnp.broadcast_to(jnp.max(column[0:share, :], axis=1, keepdims=True), (share, 128))
    column[0:share, :] = peak

    def read(rows):
        return jnp.exp(partial[x, rows, :] - wide(column[rows, :], width))

    def write(rows, value):
        spread[x, rows, :] = value.astype(bf16)
        inverse[rows, :] = fold(jnp.add, value)

    over(share, read, write, 1)
    ring = Ring(
        move,
        x,
        lambda i, h: spread.at[i] if h is None else spread.at[i, :, pl.ds(h * half, half)],
        at.on_x,
    )
    ring.begin()
    total = jnp.sum(inverse[0:share, :], axis=1, keepdims=True)
    picked = jnp.sum(third[0:share, :], axis=1, keepdims=True)
    lane = lax.broadcasted_iota(jnp.int32, (share, 128), 1)
    column[0:share, :] = jnp.where(
        lane == 0, column[0:share, :], jnp.where(lane == 1, total, picked)
    )
    stats = jnp.transpose(column[...])[0:8]
    local_peak = stats[0:1]

    arrived(ref_core)
    fetch[1].wait()
    ref_width = ref_weight.shape[1]
    ref_entry = lax.axis_index("row") * 32 + lax.axis_index("col") * 4 + y

    @pl.loop(0, 4)
    def _(k):
        for f in (0, 1):
            for h in (0, 1):
                a = refs[:, k, :, f, :, h].reshape(2 * LEN, quarter)
                b = ref_weight[(h * 2 + f) * quarter : (h * 2 + f + 1) * quarter, :]
                d = jnp.dot(a, b, preferred_element_type=f32)
                if f + h == 0:
                    ref_logits[...] = d
                else:
                    ref_logits[...] += d
        for i in range(4):
            rows = pl.ds(i * 64, 64)
            there = pl.ds(pl.multiple_of(k * 64, 64), 64)
            logits = ref_logits[rows, :]
            peak = jnp.max(logits, axis=1, keepdims=True)
            total = jnp.sum(jnp.exp(logits - peak), axis=1, keepdims=True)
            entry = (
                lax.broadcasted_iota(jnp.int32, (64, ref_width), 1) + ref_entry * ref_width
            ).astype(f32)
            picked = jnp.sum(
                jnp.where(entry == ref_wanted[i, there, 0:1], logits, 0.0), axis=1, keepdims=True
            )
            lanes = lax.broadcasted_iota(jnp.int32, (64, 128), 1)
            ref_column[i, there, :] = jnp.where(
                lanes == 0, peak, jnp.where(lanes == 1, total, picked)
            )

    for i in range(4):
        ref_stats[i] = jnp.transpose(ref_column[i])[0:8]
    copies = [
        move.start(ref_stats.at[(x + i) % 4], ref_first.at[i - 1], at.on_x(i)) for i in (1, 2, 3)
    ]
    ring.forward()
    arrived(copies)
    mine = ref_stats[x]
    for i in (0, 1, 2):
        mine = merge(mine, ref_first[i])
    both = jnp.stack([stats, mine])
    stages = [[at.other_core()], [at.on_y(i) for i in (1, 2, 3)], [at.on_z(i) for i in (1, 2, 3)]]
    slot = 0
    for s, peers in enumerate(stages):
        held[s] = both
        copies = [move.start(held.at[s], got.at[slot + k], peer) for k, peer in enumerate(peers)]
        arrived(copies)
        for k in range(len(peers)):
            both = merge(both, got[slot + k])
        slot += len(peers)

    def valid(mask, value):
        return jnp.sum(jnp.where(mask > 0, value, 0.0), axis=1, keepdims=True)

    normalizer = both[0, 0:1] + jnp.log(both[0, 1:2])
    logp = both[0, 2:3] - normalizer
    ref_logp = both[1, 2:3] - both[1, 0:1] - jnp.log(both[1, 1:2])
    mask_a, mask_b = kept_mask[x, 0:1, :], kept_mask[x, 1:2, :]
    natural = lax.broadcasted_iota(jnp.int32, (1, 2 * LEN), 1)
    mask = masks[x]
    ratio_a = valid(mask_a, logp) - valid(jnp.where(natural < LEN, mask, 0), ref_logp)
    ratio_b = valid(mask_b, logp) - valid(jnp.where(natural < LEN, 0, mask), ref_logp)
    info[x] = jnp.concatenate(
        [
            normalizer,
            local_peak,
            jnp.broadcast_to(ratio_a, (1, 2 * LEN)),
            jnp.broadcast_to(ratio_b, (1, 2 * LEN)),
            jnp.zeros((4, 2 * LEN), f32),
        ],
        axis=0,
    )
    arrived([move.start(info.at[x], info.at[x], at.on_x(i)) for i in (1, 2, 3)])
    margin = jnp.zeros((SEQS, 2 * LEN), f32)
    for s in range(SEQS):
        margin += pairs[:, s : s + 1] * info[s // 2, 2 + s % 2 : 3 + s % 2, :]
    margin *= beta_value
    log_sigmoid = jnp.minimum(margin, 0.0) - jnp.log1p(jnp.exp(-jnp.abs(margin)))
    loss[...] = jnp.broadcast_to(
        jnp.sum(log_sigmoid, axis=0, keepdims=True)[:, 0:128] * (-1.0 / SEQS), (8, 128)
    )
    weights = (
        (-loss_scale * beta_value / PAIRS)
        * jax.nn.sigmoid(-margin)
        * pairs[:, SEQS : SEQS + 1]
    )
    token_weights[...] = weights

    core_at, y_at = move.used, move.used + 8
    move.used += 32

    def core_copies(t):
        return [
            move.make(core_at + 2 * t, row_ssend.at[t], row_srecv.at[t], at.other_core()),
            move.make(core_at + 2 * t + 1, core_send.at[t % 2], core_recv.at[t], at.other_core()),
        ]

    def y_copies(t):
        copies = []
        for i in (1, 3, 2):
            k = t * 3 + i - 1
            there = (y + i) % 4
            part = y_send.at[t % 2, pl.ds(pl.multiple_of(there * count, count), count), :]
            copies.append(
                move.make(y_at + 2 * k, row_ssend.at[4 + t], row_srecv.at[4 + k], at.on_y(i))
            )
            copies.append(move.make(y_at + 2 * k + 1, part, y_recv.at[k], at.on_y(i)))
        return copies

    def out_copy(t, owner):
        return pltpu.make_async_copy(grad.at[t % 2], grad_out.at[owner], local.at[t])

    def sent(copies):
        for copy in copies:
            copy.wait_send()

    def owner_of(t):
        return (x + t + t // 2 - 2 * (t // 3)) % 4

    mine_rows = pl.ds(pl.multiple_of(y * count, count), count)

    def rows_of(owner):
        return pl.ds(pl.multiple_of(owner * count, count), count)

    @pl.loop(0, 6)
    def _(t):
        @pl.when(t == 3)
        def _():
            ring.end()

        @pl.when((t >= 2) & (t < 4))
        def _():
            sent(core_copies(t - 2))
            out_copy(t - 2, owner_of(t - 2)).wait()

        @pl.when(t < 4)
        def _():
            slot = t % 2
            owner = owner_of(t)
            mask_a, mask_b = kept_mask[owner, 0:1, :], kept_mask[owner, 1:2, :]
            weight_a = token_weights[pl.ds(2 * owner, 1), :]
            weight_b = token_weights[pl.ds(2 * owner + 1, 1), :]
            token = mask_a * weight_a + mask_b * weight_b
            factor = jnp.where(
                mask_a + mask_b > 0, token * jnp.exp(info[owner, 1:2, :] - info[owner, 0:1, :]), 0.0
            )
            column[...] = to_column(token)
            third[...] = to_column(factor)

            def read(rows):
                hits = entries(ROWS) == wide(kept_wanted[owner, rows, :], width)
                return (
                    jnp.where(hits, wide(column[rows, :], width), 0.0)
                    - wide(third[rows, :], width) * spread[owner, rows, :].astype(f32)
                ).astype(bf16)

            def write(rows, value):
                grad[slot, rows, :] = value

            over(share, read, write, 1)
            out_copy(t, owner).start()

            @pl.loop(0, width // tile)
            def _(j):
                cols = pl.ds(pl.multiple_of(j * tile, tile), tile)
                grad_full[:, cols] = jnp.dot(
                    place[owner], grad[slot, :, cols], preferred_element_type=f32
                ).astype(bf16)

            @pl.loop(0, depth // 256)
            def _(j):
                cols = pl.ds(pl.multiple_of(j * 256, 256), 256)
                rows_all[slot, :, :, cols] = lax.dot_general(
                    grad_full[...],
                    weight[cols, :],
                    (((1,), (1,)), ((), ())),
                    preferred_element_type=f32,
                ).reshape(2, LEN, 256)

            def write(rows, code):
                core_send[slot, rows, :] = code

            row_ssend[t] = encode(LEN, lambda rows: rows_all[slot, 1 - c, rows, :], write)
            for copy in core_copies(t):
                copy.start()

        @pl.when((t >= 3) & (t < 5))
        def _():
            sent(y_copies(t - 3))

        @pl.when((t >= 1) & (t < 5))
        def _():
            u = t - 1
            slot = u % 2
            for copy in core_copies(u):
                copy.wait_recv()
            third[...] = to_column(row_srecv[u, 0:1, :])

            def read(rows):
                return rows_all[slot, c, rows, :] + decode(core_recv[u, rows, :], third[rows, :])

            def store(rows, value=None):
                if value is None:
                    return rows_all[slot, c, rows, :]
                rows_all[slot, c, rows, :] = value

            def write(rows, code):
                y_send[slot, rows, :] = code

            row_ssend[4 + u] = encode(LEN, read, write, store)
            for copy in y_copies(u):
                copy.start()
            z_sum[rows_of(owner_of(u)), :] = rows_all[slot, c, mine_rows, :]

        @pl.when(t >= 2)
        def _():
            v = t - 2
            for copy in y_copies(v):
                copy.wait_recv()
            total = z_sum[rows_of(owner_of(v)), :]
            for i in range(3):
                k = v * 3 + i
                column[...] = to_column(row_srecv[4 + k, 0:1, :])
                total += decode(y_recv[k], column[mine_rows, :])
            z_sum[rows_of(owner_of(v)), :] = total

    for t in (2, 3):
        sent(core_copies(t))
        sent(y_copies(t))
        out_copy(t, owner_of(t)).wait()

    def write(rows, code):
        z_send[rows, :] = code

    row_ssend[8] = encode(LEN, lambda rows: z_sum[rows, :], write)
    copies = []
    for i in (1, 3, 2):
        there = (z + i) % 4
        copies.append(move.start(row_ssend.at[8], row_srecv.at[16 + i - 1], at.on_z(i)))
        part = z_send.at[pl.ds(pl.multiple_of(there * count, count), count), :]
        copies.append(move.start(part, z_recv.at[i - 1], at.on_z(i)))
    arrived(copies)
    here = pl.ds(pl.multiple_of(z * count, count), count)
    total = z_sum[here, :]
    for i in range(3):
        column[...] = to_column(row_srecv[16 + i, 0:1, :])
        total += decode(z_recv[i], column[here, :])
    rows_out[...] = total
    move.finish()


def fused(index, share, states, others, weight, ref_weight, masks, wanted, pairs):
    vmem = pl.BlockSpec(memory_space=pltpu.VMEM)
    count, depth = states.shape
    width = weight.shape[1]
    ref_rows, ref_depth = others.shape
    quarter = ref_depth // 4
    f32, bf16, i16 = jnp.float32, jnp.bfloat16, jnp.int16
    lanes = 2 * LEN
    copies = 128
    return pl.pallas_call(
        fused_kernel,
        name="fused_%d" % share,
        out_shape=(
            jax.ShapeDtypeStruct((8, 128), f32),
            jax.ShapeDtypeStruct((count, depth), f32),
            jax.ShapeDtypeStruct((4, share, width), bf16),
            jax.ShapeDtypeStruct((4, share, depth), bf16),
        ),
        in_specs=[vmem, vmem, pl.BlockSpec(memory_space=pl.ANY), pl.BlockSpec(memory_space=pl.ANY)]
        + [vmem] * 3,
        out_specs=(vmem, vmem, pl.BlockSpec(memory_space=pl.ANY), vmem),
        scratch_shapes=[
            pltpu.VMEM(weight.shape, bf16),
            pltpu.VMEM(ref_weight.shape, bf16),
            pltpu.VMEM((4, 2, 4, count, depth), bf16),
            pltpu.VMEM((2, ref_rows, ref_depth // 2), f32),
            pltpu.VMEM((ref_rows, ref_depth // 2), f32),
            pltpu.VMEM((4, 4, 2, 2, 2, 2, 2 * ref_rows, quarter), bf16),
            pltpu.VMEM((4, share, width), f32),
            pltpu.VMEM((4, share, width // 2), i16),
            pltpu.VMEM((6, share, width // 2), i16),
            pltpu.VMEM((6, 8, lanes), f32),
            pltpu.VMEM((6, 8, lanes), f32),
            pltpu.VMEM((lanes, 128), f32),
            pltpu.VMEM((lanes, 128), f32),
            pltpu.VMEM((lanes, 128), f32),
            pltpu.VMEM((4, share, 128), f32),
            pltpu.VMEM((4, share, lanes), bf16),
            pltpu.VMEM((4, lanes, share), bf16),
            pltpu.VMEM((4, 8, lanes), f32),
            pltpu.VMEM((4, share, width), bf16),
            pltpu.VMEM((lanes, ref_weight.shape[1]), f32),
            pltpu.VMEM((4, lanes, 128), f32),
            pltpu.VMEM((4, lanes, 128), f32),
            pltpu.VMEM((4, 8, lanes), f32),
            pltpu.VMEM((3, 8, lanes), f32),
            pltpu.VMEM((3, 2, 8, lanes), f32),
            pltpu.VMEM((7, 2, 8, lanes), f32),
            pltpu.VMEM((4, 8, lanes), f32),
            pltpu.VMEM((8, lanes), f32),
            pltpu.VMEM((2, share, width), bf16),
            pltpu.VMEM((lanes, width), bf16),
            pltpu.VMEM((2, 2, LEN, depth), f32),
            pltpu.VMEM((2, LEN, depth), i16),
            pltpu.VMEM((4, LEN, depth), i16),
            pltpu.VMEM((2, LEN, depth), i16),
            pltpu.VMEM((12, count, depth), i16),
            pltpu.VMEM((LEN, depth), i16),
            pltpu.VMEM((3, count, depth), i16),
            pltpu.VMEM((LEN, depth), f32),
            pltpu.VMEM((9, 8, lanes), f32),
            pltpu.VMEM((19, 8, lanes), f32),
            pltpu.SemaphoreType.DMA((copies,)),
            pltpu.SemaphoreType.DMA((copies,)),
            pltpu.SemaphoreType.DMA((6,)),
        ],
        compiler_params=pltpu.CompilerParams(
            collective_id=index, has_side_effects=True, vmem_limit_bytes=VMEM_LIMIT
        ),
    )(states, others, weight, ref_weight, masks, wanted, pairs)


def weight_kernel(states, grad, out, turned):
    @pl.when(pl.program_id(0) == 0)
    def _():
        turned[...] = jnp.transpose(states[...])

    out[...] = jnp.dot(turned[...], grad[...], preferred_element_type=jnp.float32)


def weight_gradient(states, grad):
    tokens, depth = states.shape
    width = grad.shape[1]
    tile = 512
    return pl.pallas_call(
        weight_kernel,
        name="weight_gradient",
        grid=(width // tile,),
        out_shape=jax.ShapeDtypeStruct((depth, width), jnp.float32),
        in_specs=[
            pl.BlockSpec((tokens, depth), lambda j: (0, 0)),
            pl.BlockSpec((tokens, tile), lambda j: (0, j)),
        ],
        out_specs=pl.BlockSpec((depth, tile), lambda j: (0, j)),
        scratch_shapes=[pltpu.VMEM((depth, tokens), states.dtype)],
        compiler_params=pltpu.CompilerParams(vmem_limit_bytes=VMEM_LIMIT),
    )(states, grad)


def on_device(
    policy_states,
    reference_states,
    policy_weight,
    reference_weight,
    targets,
    response_mask,
    pair_index,
    chosen_flag,
):
    masks = response_mask.reshape(4, 1, 2 * LEN)
    wanted = targets.reshape(4, 1, 2 * LEN)
    sign = (2 * chosen_flag - 1).astype(jnp.float32)
    same = (pair_index[:, None] == pair_index[None, :]).astype(jnp.float32)
    pairs = jnp.concatenate(
        [same * sign[None, :], sign[:, None], jnp.zeros((SEQS, 128 - SEQS - 1), jnp.float32)], axis=1
    )

    def run(index):
        def branch(*operands):
            loss, grad_states, grad, states = fused(index, SIZES[index], *operands)
            grad_weight = weight_gradient(
                states.reshape(-1, states.shape[2]), grad.reshape(-1, grad.shape[2])
            )
            return (loss[0, 0], grad_states, grad_weight)

        return branch

    longest = jnp.max(jnp.sum(response_mask.reshape(4, 2 * LEN), axis=1))
    size = sum((longest > s).astype(jnp.int32) for s in SIZES[:-1])
    return lax.switch(
        size,
        [run(i) for i in range(len(SIZES))],
        policy_states,
        reference_states,
        policy_weight,
        reference_weight,
        masks,
        wanted,
        pairs,
    )


def solution(mesh):
    in_specs = (
        P(("col", "depth"), "row"),
        P(("row", "col", "depth"), None),
        P("row", ("col", "depth")),
        P(None, ("row", "col", "depth")),
        P(),
        P(),
        P(),
        P(),
    )
    out_specs = (P(), P(("col", "depth"), "row"), P("row", ("col", "depth")))
    return jax.shard_map(
        on_device, mesh=mesh, in_specs=in_specs, out_specs=out_specs, check_vma=False
    )
```

profile of v0, /device:TPU:0, one launch (start us, length us, event | category | flops | bytes accessed | tf_op | source)
XLA Modules:
  0.0 157.0 jit_solution(15849711996345289477)
XLA Ops:
  0.6 0.1 pad.2.clone
  0.7 0.7 add_convert_fusion
  1.4 0.8 compare_select_fusion
  2.2 0.1 copy.26
  2.3 0.1 maximum_maximum_fusion
  2.3 0.7 reshape.30
  3.0 0.1 reduce_sum.9
  3.1 0.6 reduce_max.9
  4.4 151.3 %conditional.1 = (f32[32,1280]{1,0:T(8,128)S(1)}, f32[1280,2560]{1,0:T(8,128)}, f32[8,128]{1,0:T(8,128)S(1)}) conditional(s32[]{:T(128)} %clamp.3, (bf16[32,1280]{1,0:T(8,128)(2,1)}, bf16[8,5120]{1,0:T(8,128)(2,1)}, bf16[1280,2560]{1,0:T(8,128)(2,1)}, bf16[5120,640]{1,0:T(8,128)(2,1)}, s32[1024]{0:T(1024)}, /*index=5*/s32[1024]{0:T(1024)}, ...), branch_computations={%region_2.0_spmd, %region_3.0_spmd} | conditional | bytes 24 | solution.py:896
  4.5 140.6 %fused_176.1 = (f32[8,128]{1,0:T(8,128)S(1)}, f32[32,1280]{1,0:T(8,128)S(1)}, bf16[4,176,2560]{2,1,0:T(8,128)(2,1)}, bf16[4,176,1280]{2,1,0:T(8,128)(2,1)}) custom-call(bf16[32,1280]{1,0:T(8,128)(2,1)} %get-tuple-element.67.own, bf16[8,5120]{1,0:T(8,128)(2,1)} %get-tuple-element.69.ref_own, bf16[1280,2560]{1,0:T(8,128)(2,1)} %get-tuple-element.71.weight_in, ...), custom_call_target="tpu_custom_call" | custom-call | tf_op jit(solution)/shard_map/cond/branch_0_fun/fused_176/pallas_call | solution.py:776
  145.1 10.7 %weight_gradient.2 = f32[1280,2560]{1,0:T(8,128)} custom-call(bf16[704,1280]{1,0:T(8,128)(2,1)} %bitcast.14, bf16[704,2560]{1,0:T(8,128)(2,1)} %bitcast.12), custom_call_target="tpu_custom_call" | custom-call | tf_op jit(solution)/shard_map/cond/branch_0_fun/weight_gradient/pallas_call | solution.py:851
  155.8 0.5 slice.6
  156.3 0.7 copy.34
  (1 shorter events, 0.0 us)
where the time goes:
time: 157 us
  Pallas kernels  151 us (96%)
  other arithmetic  2.29 us (1%)
  local copies, waits for them, and re-layouts  2.03 us (1%)
    pallas_call x1, Pallas kernels, fused(): pl.pallas_call(fused_kernel, name='fused_%d' % share, out_shape=(jax.Shap...  141 us
    pallas_call x1, Pallas kernels, weight_gradient(): pl.pallas_call(weight_kernel, name='weight_gradient', grid=(width // tile...  10.7 us

commit v1 on v0

--- a/solution.py
+++ b/solution.py
@@ -20,16 +20,6 @@
 MESH = pl.DeviceIdType.MESH
 VMEM_LIMIT = 62 * 1024 * 1024
 ROWS = 16
-
-
-def preference(ratio, pair_index, chosen_flag):
-    sign = (2 * chosen_flag - 1).astype(jnp.float32)
-    member = pair_index[:, None] == jnp.arange(PAIRS, dtype=jnp.int32)[None, :]
-    margin = jnp.sum(jnp.where(member, (sign * ratio)[:, None], 0.0), axis=0)
-    loss = -jnp.mean(jax.nn.log_sigmoid(beta_value * margin))
-    slope = -loss_scale * beta_value / PAIRS * jax.nn.sigmoid(-beta_value * margin)
-    weights = sign * jnp.sum(jnp.where(member, slope[None, :], 0.0), axis=1)
-    return (loss, weights)
 
 
 class Place:
@@ -110,6 +100,9 @@
         part = self.view((self.me + 1) % 4, 1)
         self.far_left = self.mover.start(part, part, self.peer(3))
 
+    def copies(self):
+        return [self.right, self.left, self.far_right, self.far_left]
+
     def end(self):
         self.far_right.wait_recv()
         self.far_left.wait_recv()
@@ -167,16 +160,18 @@
     ref_weight_in,
     masks,
     wanted,
-    pairs,
+    pair_index,
+    chosen_flag,
     loss,
     rows_out,
     grad_out,
+    turned_out,
     kept,
+    pairs,
+    turned,
     weight,
     ref_weight,
     gathered,
-    ref_half,
-    ref_got,
     refs,
     partial,
     qsend,
@@ -193,21 +188,14 @@
     spread,
     ref_logits,
     ref_column,
-    ref_wanted,
     ref_stats,
-    ref_first,
     held,
     got,
     info,
     token_weights,
-    grad,
     grad_full,
     rows_all,
-    core_send,
-    core_recv,
     y_send,
-    y_recv,
-    z_send,
     z_recv,
     z_sum,
     row_ssend,
@@ -223,8 +211,8 @@
     half = width // 2
     f32, bf16 = jnp.float32, jnp.bfloat16
     fetch = [
-        pltpu.make_async_copy(weight_in, weight, local.at[4]),
-        pltpu.make_async_copy(ref_weight_in, ref_weight, local.at[5]),
+        pltpu.make_async_copy(weight_in, weight, local.at[10]),
+        pltpu.make_async_copy(ref_weight_in, ref_weight, local.at[11]),
     ]
     for copy in fetch:
         copy.start()
@@ -245,19 +233,23 @@
     side, pair = y % 2, y // 2
     ref_depth = ref_own.shape[1]
     quarter = ref_depth // 4
-    for k in (0, 1):
-        ref_half[k] = ref_own[:, k * 2 * quarter : (k + 1) * 2 * quarter].astype(f32)
-    swap = move.start(ref_half.at[1 - side], ref_got, at.partner_y())
+    for k in range(4):
+        z_sum[8 * k : 8 * k + 8, :] = ref_own[:, k * quarter : (k + 1) * quarter].astype(f32)
+    swap = move.start(
+        z_sum.at[pl.ds(pl.multiple_of(16 - 16 * side, 16), 16), :],
+        z_sum.at[32:48, :],
+        at.partner_y(),
+    )
     column[...] = jnp.zeros_like(column)
     first_y.forward()
     first_z.forward()
     swap.wait_recv()
-    mine, theirs = ref_half[side], ref_got[...]
-    block = jnp.concatenate(
-        [jnp.where(side == 0, mine, theirs), jnp.where(side == 0, theirs, mine)], axis=0
-    ).astype(bf16)
+    mine, theirs = z_sum[pl.ds(pl.multiple_of(16 * side, 16), 16), :], z_sum[32:48, :]
     for f in (0, 1):
-        refs[x, z, c, f, pair, side] = block[:, f * quarter : (f + 1) * quarter]
+        a, b = mine[8 * f : 8 * f + 8], theirs[8 * f : 8 * f + 8]
+        block = [jnp.where(side == 0, a, b), jnp.where(side == 0, b, a)]
+        refs[x, z, c, f, pair, side] = jnp.concatenate(block, axis=0).astype(bf16)
+    move.sent(swap)
     ref_x = Ring(
         move,
         x,
@@ -269,6 +261,7 @@
     ref_yz = Ring(move, z, lambda i, h: refs.at[span(h, 4), i, c, 0], at.on_z)
     ref_zy = Ring(move, y, lambda i, h: refs.at[span(h, 4), :, c, 1, i // 2, i % 2], at.on_y)
     ref_core = []
+    ref_rings = [ref_x, ref_y, ref_z, ref_yz, ref_zy]
 
     def to_core(ring, i):
         part = ring.view((ring.me + i) % 4, None)
@@ -313,7 +306,16 @@
         return a, (i < len_a + len_b).astype(f32) - a
 
     for k in range(4):
-        ref_wanted[k] = to_column(wanted[k].astype(f32))
+        ref_column[k] = to_column(wanted[k].astype(f32))
+
+    lane = lax.broadcasted_iota(jnp.int32, (1, 128), 1)
+    signs = [(2 * chosen_flag[s] - 1).astype(f32) for s in range(SEQS)]
+    for s in range(SEQS):
+        row = jnp.where(lane == SEQS, signs[s], 0.0)
+        for other in range(SEQS):
+            sign = jnp.where(pair_index[s] == pair_index[other], signs[other], 0.0)
+            row += jnp.where(lane == other, sign, 0.0)
+        pairs[s : s + 1, :] = row
 
     @pl.loop(0, 4)
     def _(o):
@@ -323,7 +325,8 @@
         target = jnp.sum(jnp.where(here, wanted[o].astype(f32), 0.0), axis=1, keepdims=True)
         kept_wanted[o] = jnp.broadcast_to(target, (share, 128))
         to = source(o, lax.broadcasted_iota(jnp.int32, (1, share), 1))
-        place[o] = (lax.broadcasted_iota(jnp.int32, (2 * LEN, share), 0) == to).astype(bf16)
+        row = lax.broadcasted_iota(jnp.int32, (2 * KEEP, share), 0) + SKIP
+        place[o] = (row + jnp.where(row >= LEN, SKIP, 0) == to).astype(bf16)
         mask_a, mask_b = kept_masks(o)
         kept_mask[o, 0:1, :] = mask_a
         kept_mask[o, 1:2, :] = mask_b
@@ -335,11 +338,15 @@
     ref_x.forward()
     then_z.end()
     share_core(then_z, (2,))
-    then_y.end()
-    share_core(then_y, (2,))
     ref_x.end()
     ref_y.begin()
     ref_z.begin()
+    then_y.end()
+    share_core(then_y, (2,))
+    ref_logits[...] = jnp.zeros_like(ref_logits)
+    rows_all[:, :, 0:SKIP, :] = jnp.zeros((2, 2, SKIP, depth), f32)
+    ref_y.forward()
+    ref_z.forward()
     fetch[0].wait()
     for copy in own_core:
         copy.wait_recv()
@@ -429,19 +436,44 @@
     product(across)
     r0 = pack(0, across, 0, right)
     l0 = pack(3, across, 1, left)
-    ref_y.forward()
-    ref_z.forward()
-    product(after)
-    r1 = pack(1, after, 1, right)
-    product(before)
-    l1 = pack(4, before, 0, left)
     ref_y.end()
     ref_yz.begin()
     to_core(ref_yz, 0)
     ref_z.end()
     ref_zy.begin()
     to_core(ref_zy, 0)
+    product(after)
+    r1 = pack(1, after, 1, right)
+    product(before)
+    l1 = pack(4, before, 0, left)
     product(x)
+
+    def ref_product(e):
+        step = e + e // 2 - 2 * (e // 3)
+        plane, row = (z + step) % 4, (y + step) % 4
+        part = jnp.zeros((2 * LEN, ref_weight.shape[1]), f32)
+        for h in (0, 1):
+            part += jnp.dot(
+                refs[:, plane, :, 0, :, h].reshape(2 * LEN, quarter),
+                ref_weight[2 * h * quarter : (2 * h + 1) * quarter, :],
+                preferred_element_type=f32,
+            )
+        ref_logits[:, plane] += part.reshape(4, 2, 2, 16, ref_weight.shape[1])
+        there = pl.ds(pl.multiple_of((row % 2 * 2 + 1) * quarter, quarter), quarter)
+
+        @pl.loop(0, 2)
+        def _(i):
+            half_x = pl.ds(2 * i, 2)
+            part = jnp.dot(
+                refs[half_x, :, :, 1, row // 2, row % 2].reshape(2 * LEN, quarter),
+                ref_weight[there, :],
+                preferred_element_type=f32,
+            )
+            ref_logits[half_x, :, :, row // 2] += part.reshape(2, 4, 2, 16, ref_weight.shape[1])
+
+    fetch[1].wait()
+    arrived(ref_core[0:2])
+    ref_product(0)
     arrived(r0)
     move.sent(r0[1])
     r2 = pack(2, after, 0, right, add=0)
@@ -462,6 +494,12 @@
     to_core(ref_yz, 2)
     ref_zy.end()
     to_core(ref_zy, 2)
+    arrived(ref_core[2:6])
+
+    @pl.loop(1, 3)
+    def _(e):
+        ref_product(e)
+
     arrived(r2)
     arrived(l2)
     column[...] = to_column(srecv[2, 0:1, :])
@@ -510,85 +548,79 @@
     stats = jnp.transpose(column[...])[0:8]
     local_peak = stats[0:1]
 
-    arrived(ref_core)
-    fetch[1].wait()
+    arrived(ref_core[6:8])
+    ref_product(3)
     ref_width = ref_weight.shape[1]
     ref_entry = lax.axis_index("row") * 32 + lax.axis_index("col") * 4 + y
 
-    @pl.loop(0, 4)
+    @pl.loop(0, 16)
     def _(k):
-        for f in (0, 1):
-            for h in (0, 1):
-                a = refs[:, k, :, f, :, h].reshape(2 * LEN, quarter)
-                b = ref_weight[(h * 2 + f) * quarter : (h * 2 + f + 1) * quarter, :]
-                d = jnp.dot(a, b, preferred_element_type=f32)
-                if f + h == 0:
-                    ref_logits[...] = d
-                else:
-                    ref_logits[...] += d
-        for i in range(4):
-            rows = pl.ds(i * 64, 64)
-            there = pl.ds(pl.multiple_of(k * 64, 64), 64)
-            logits = ref_logits[rows, :]
-            peak = jnp.max(logits, axis=1, keepdims=True)
-            total = jnp.sum(jnp.exp(logits - peak), axis=1, keepdims=True)
-            entry = (
-                lax.broadcasted_iota(jnp.int32, (64, ref_width), 1) + ref_entry * ref_width
-            ).astype(f32)
-            picked = jnp.sum(
-                jnp.where(entry == ref_wanted[i, there, 0:1], logits, 0.0), axis=1, keepdims=True
-            )
-            lanes = lax.broadcasted_iota(jnp.int32, (64, 128), 1)
-            ref_column[i, there, :] = jnp.where(
-                lanes == 0, peak, jnp.where(lanes == 1, total, picked)
-            )
+        i, j = k // 4, k % 4
+        rows = pl.ds(pl.multiple_of(j * 64, 64), 64)
+        logits = ref_logits[i, j].reshape(64, ref_width)
+        peak = jnp.max(logits, axis=1, keepdims=True)
+        total = jnp.sum(jnp.exp(logits - peak), axis=1, keepdims=True)
+        entry = (
+            lax.broadcasted_iota(jnp.int32, (64, ref_width), 1) + ref_entry * ref_width
+        ).astype(f32)
+        picked = jnp.sum(
+            jnp.where(entry == ref_column[i, rows, 0:1], logits, 0.0), axis=1, keepdims=True
+        )
+        lanes = lax.broadcasted_iota(jnp.int32, (64, 128), 1)
+        ref_column[i, rows, :] = jnp.where(lanes == 0, peak, jnp.where(lanes == 1, total, picked))
 
     for i in range(4):
         ref_stats[i] = jnp.transpose(ref_column[i])[0:8]
-    copies = [
-        move.start(ref_stats.at[(x + i) % 4], ref_first.at[i - 1], at.on_x(i)) for i in (1, 2, 3)
-    ]
-    ring.forward()
-    arrived(copies)
-    mine = ref_stats[x]
-    for i in (0, 1, 2):
-        mine = merge(mine, ref_first[i])
-    both = jnp.stack([stats, mine])
+    for copy in ref_core + [ring_copy for r in ref_rings for ring_copy in r.copies()]:
+        move.sent(copy)
+
+    for copies in (r1, l1, r2, l2):
+        move.sent(copies[1])
+
+    every = jnp.concatenate([stats[None], ref_stats[...]], axis=0)
     stages = [[at.other_core()], [at.on_y(i) for i in (1, 2, 3)], [at.on_z(i) for i in (1, 2, 3)]]
     slot = 0
     for s, peers in enumerate(stages):
-        held[s] = both
+        held[s] = every
         copies = [move.start(held.at[s], got.at[slot + k], peer) for k, peer in enumerate(peers)]
         arrived(copies)
         for k in range(len(peers)):
-            both = merge(both, got[slot + k])
+            every = merge(every, got[slot + k])
         slot += len(peers)
 
     def valid(mask, value):
-        return jnp.sum(jnp.where(mask > 0, value, 0.0), axis=1, keepdims=True)
-
-    normalizer = both[0, 0:1] + jnp.log(both[0, 1:2])
-    logp = both[0, 2:3] - normalizer
-    ref_logp = both[1, 2:3] - both[1, 0:1] - jnp.log(both[1, 1:2])
-    mask_a, mask_b = kept_mask[x, 0:1, :], kept_mask[x, 1:2, :]
-    natural = lax.broadcasted_iota(jnp.int32, (1, 2 * LEN), 1)
-    mask = masks[x]
-    ratio_a = valid(mask_a, logp) - valid(jnp.where(natural < LEN, mask, 0), ref_logp)
-    ratio_b = valid(mask_b, logp) - valid(jnp.where(natural < LEN, 0, mask), ref_logp)
-    info[x] = jnp.concatenate(
+        return jnp.sum(jnp.where(mask > 0, value, 0.0), axis=-1, keepdims=True)
+
+    normalizer = every[0, 0:1] + jnp.log(every[0, 1:2])
+    logp = every[0, 2:3] - normalizer
+    info[x, 0] = jnp.concatenate(
         [
             normalizer,
             local_peak,
-            jnp.broadcast_to(ratio_a, (1, 2 * LEN)),
-            jnp.broadcast_to(ratio_b, (1, 2 * LEN)),
+            jnp.broadcast_to(valid(kept_mask[x, 0:1, :], logp), (1, 2 * LEN)),
+            jnp.broadcast_to(valid(kept_mask[x, 1:2, :], logp), (1, 2 * LEN)),
             jnp.zeros((4, 2 * LEN), f32),
         ],
         axis=0,
     )
-    arrived([move.start(info.at[x], info.at[x], at.on_x(i)) for i in (1, 2, 3)])
+    info[x, 1:5] = every[1:5]
+    info_copies = [move.start(info.at[x], info.at[x], at.on_x(i)) for i in (1, 2, 3)]
+    ring.forward()
+    arrived(info_copies)
+    merged = info[0, 1:5]
+    for i in (1, 2, 3):
+        merged = merge(merged, info[i, 1:5])
+    ref_logp = merged[:, 2:3] - merged[:, 0:1] - jnp.log(merged[:, 1:2])
+    natural = lax.broadcasted_iota(jnp.int32, (4, 1, 2 * LEN), 2)
+    mask = masks[...]
+    ref_sums = (
+        valid(jnp.where(natural < LEN, mask, 0), ref_logp),
+        valid(jnp.where(natural < LEN, 0, mask), ref_logp),
+    )
     margin = jnp.zeros((SEQS, 2 * LEN), f32)
     for s in range(SEQS):
-        margin += pairs[:, s : s + 1] * info[s // 2, 2 + s % 2 : 3 + s % 2, :]
+        ratio = info[s // 2, 0, 2 + s % 2 : 3 + s % 2, :] - ref_sums[s % 2][s // 2]
+        margin += pairs[:, s : s + 1] * ratio
     margin *= beta_value
     log_sigmoid = jnp.minimum(margin, 0.0) - jnp.log1p(jnp.exp(-jnp.abs(margin)))
     loss[...] = jnp.broadcast_to(
@@ -601,13 +633,23 @@
     )
     token_weights[...] = weights
 
-    core_at, y_at = move.used, move.used + 8
-    move.used += 32
+    core_at, y_at, z_at = move.used, move.used + 8, move.used + 32
+    move.used += 38
+
+    def z_copies():
+        copies = []
+        for i in (1, 3, 2):
+            there = (z + i) % 4
+            k = z_at + 2 * i - 2
+            copies.append(move.make(k, row_ssend.at[8], row_srecv.at[16 + i - 1], at.on_z(i)))
+            part = y_send.at[0, pl.ds(pl.multiple_of(there * count, count), count), :]
+            copies.append(move.make(k + 1, part, z_recv.at[i - 1], at.on_z(i)))
+        return copies
 
     def core_copies(t):
         return [
             move.make(core_at + 2 * t, row_ssend.at[t], row_srecv.at[t], at.other_core()),
-            move.make(core_at + 2 * t + 1, core_send.at[t % 2], core_recv.at[t], at.other_core()),
+            move.make(core_at + 2 * t + 1, qrecv.at[4 + t % 2, 0:LEN, :], qrecv.at[t, 0:LEN, :], at.other_core()),
         ]
 
     def y_copies(t):
@@ -619,11 +661,38 @@
             copies.append(
                 move.make(y_at + 2 * k, row_ssend.at[4 + t], row_srecv.at[4 + k], at.on_y(i))
             )
-            copies.append(move.make(y_at + 2 * k + 1, part, y_recv.at[k], at.on_y(i)))
+            into = qsend.at[t, (i - 1) * count : i * count, :]
+            copies.append(move.make(y_at + 2 * k + 1, part, into, at.on_y(i)))
         return copies
 
-    def out_copy(t, owner):
-        return pltpu.make_async_copy(grad.at[t % 2], grad_out.at[owner], local.at[t])
+    def grad_part(owner, f, cols):
+        return refs[owner, :, :, f, :, 0, :, cols].reshape(2 * LEN, -1)[0:share]
+
+    def out_copies(owner):
+        return [
+            pltpu.make_async_copy(
+                refs.at[owner, :, :, f, :, 0],
+                grad_out.at[owner, :, :, :, :, pl.ds(f * quarter, quarter)],
+                local.at[2 * owner + f],
+            )
+            for f in (0, 1)
+        ]
+
+    def turned_copy(k):
+        rows = pl.ds(pl.multiple_of(k * 2 * LEN, 2 * LEN), 2 * LEN)
+        return pltpu.make_async_copy(
+            turned, turned_out.at[rows, :], local.at[8]
+        )
+
+    def turn(k):
+        rows = pl.ds(pl.multiple_of(k * 2 * LEN, 2 * LEN), 2 * LEN)
+
+        @pl.when(k >= 1)
+        def _():
+            turned_copy(k - 1).wait()
+
+        turned[...] = jnp.transpose(kept[:, :, rows].reshape(4 * share, 2 * LEN))
+        turned_copy(k).start()
 
     def sent(copies):
         for copy in copies:
@@ -646,7 +715,6 @@
         @pl.when((t >= 2) & (t < 4))
         def _():
             sent(core_copies(t - 2))
-            out_copy(t - 2, owner_of(t - 2)).wait()
 
         @pl.when(t < 4)
         def _():
@@ -657,7 +725,7 @@
             weight_b = token_weights[pl.ds(2 * owner + 1, 1), :]
             token = mask_a * weight_a + mask_b * weight_b
             factor = jnp.where(
-                mask_a + mask_b > 0, token * jnp.exp(info[owner, 1:2, :] - info[owner, 0:1, :]), 0.0
+                mask_a + mask_b > 0, token * jnp.exp(info[owner, 0, 1:2, :] - info[owner, 0, 0:1, :]), 0.0
             )
             column[...] = to_column(token)
             third[...] = to_column(factor)
@@ -669,31 +737,37 @@
                     - wide(third[rows, :], width) * spread[owner, rows, :].astype(f32)
                 ).astype(bf16)
 
-            def write(rows, value):
-                grad[slot, rows, :] = value
-
-            over(share, read, write, 1)
-            out_copy(t, owner).start()
-
-            @pl.loop(0, width // tile)
-            def _(j):
-                cols = pl.ds(pl.multiple_of(j * tile, tile), tile)
-                grad_full[:, cols] = jnp.dot(
-                    place[owner], grad[slot, :, cols], preferred_element_type=f32
-                ).astype(bf16)
+            @pl.loop(0, share // ROWS)
+            def _(r):
+                value = read(pl.ds(pl.multiple_of(r * ROWS, ROWS), ROWS))
+                refs[owner, r // 4, r // 2 % 2, 0, r % 2, 0] = value[:, 0:half]
+                refs[owner, r // 4, r // 2 % 2, 1, r % 2, 0] = value[:, half:]
+
+            for copy in out_copies(owner):
+                copy.start()
+
+            for f in (0, 1):
+
+                @pl.loop(0, half // tile)
+                def _(j):
+                    cols = pl.ds(pl.multiple_of(j * tile, tile), tile)
+                    there = pl.ds(pl.multiple_of(f * half + j * tile, tile), tile)
+                    grad_full[:, there] = jnp.dot(
+                        place[owner], grad_part(owner, f, cols), preferred_element_type=f32
+                    ).astype(bf16)
 
             @pl.loop(0, depth // 256)
             def _(j):
                 cols = pl.ds(pl.multiple_of(j * 256, 256), 256)
-                rows_all[slot, :, :, cols] = lax.dot_general(
+                rows_all[slot, :, SKIP:LEN, cols] = lax.dot_general(
                     grad_full[...],
                     weight[cols, :],
                     (((1,), (1,)), ((), ())),
                     preferred_element_type=f32,
-                ).reshape(2, LEN, 256)
+                ).reshape(2, KEEP, 256)
 
             def write(rows, code):
-                core_send[slot, rows, :] = code
+                qrecv[4 + slot, rows, :] = code
 
             row_ssend[t] = encode(LEN, lambda rows: rows_all[slot, 1 - c, rows, :], write)
             for copy in core_copies(t):
@@ -712,7 +786,7 @@
             third[...] = to_column(row_srecv[u, 0:1, :])
 
             def read(rows):
-                return rows_all[slot, c, rows, :] + decode(core_recv[u, rows, :], third[rows, :])
+                return rows_all[slot, c, rows, :] + decode(qrecv[u, rows, :], third[rows, :])
 
             def store(rows, value=None):
                 if value is None:
@@ -736,35 +810,48 @@
             for i in range(3):
                 k = v * 3 + i
                 column[...] = to_column(row_srecv[4 + k, 0:1, :])
-                total += decode(y_recv[k], column[mine_rows, :])
+                code = qsend[v, i * count : (i + 1) * count, :]
+                total += decode(code, column[mine_rows, :])
             z_sum[rows_of(owner_of(v)), :] = total
 
-    for t in (2, 3):
-        sent(core_copies(t))
-        sent(y_copies(t))
-        out_copy(t, owner_of(t)).wait()
-
-    def write(rows, code):
-        z_send[rows, :] = code
-
-    row_ssend[8] = encode(LEN, lambda rows: z_sum[rows, :], write)
-    copies = []
-    for i in (1, 3, 2):
-        there = (z + i) % 4
-        copies.append(move.start(row_ssend.at[8], row_srecv.at[16 + i - 1], at.on_z(i)))
-        part = z_send.at[pl.ds(pl.multiple_of(there * count, count), count), :]
-        copies.append(move.start(part, z_recv.at[i - 1], at.on_z(i)))
-    arrived(copies)
+        @pl.when(t == 5)
+        def _():
+            for u in (2, 3):
+                sent(core_copies(u))
+                sent(y_copies(u))
+
+            def write(rows, code):
+                y_send[0, rows, :] = code
+
+            row_ssend[8] = encode(LEN, lambda rows: z_sum[rows, :], write)
+            for copy in z_copies():
+                copy.start()
+
+        @pl.when(t >= 3)
+        def _():
+            start = 2 * (t - 3)
+
+            @pl.loop(start, jnp.minimum(start + 2, depth // (2 * LEN)))
+            def _(k):
+                turn(k)
+
+    for copy in z_copies():
+        copy.wait_recv()
     here = pl.ds(pl.multiple_of(z * count, count), count)
     total = z_sum[here, :]
     for i in range(3):
         column[...] = to_column(row_srecv[16 + i, 0:1, :])
         total += decode(z_recv[i], column[here, :])
     rows_out[...] = total
+    sent(z_copies())
+    turned_copy(depth // (2 * LEN) - 1).wait()
+    for owner in range(4):
+        for copy in out_copies(owner):
+            copy.wait()
     move.finish()
 
 
-def fused(index, share, states, others, weight, ref_weight, masks, wanted, pairs):
+def fused(index, share, states, others, weight, ref_weight, masks, wanted, pair_index, chosen):
     vmem = pl.BlockSpec(memory_space=pltpu.VMEM)
     count, depth = states.shape
     width = weight.shape[1]
@@ -779,18 +866,21 @@
         out_shape=(
             jax.ShapeDtypeStruct((8, 128), f32),
             jax.ShapeDtypeStruct((count, depth), f32),
-            jax.ShapeDtypeStruct((4, share, width), bf16),
-            jax.ShapeDtypeStruct((4, share, depth), bf16),
+            jax.ShapeDtypeStruct((4, 4, 2, 2, 2 * ref_rows, width), bf16),
+            jax.ShapeDtypeStruct((depth, 4 * share), bf16),
         ),
-        in_specs=[vmem, vmem, pl.BlockSpec(memory_space=pl.ANY), pl.BlockSpec(memory_space=pl.ANY)]
-        + [vmem] * 3,
-        out_specs=(vmem, vmem, pl.BlockSpec(memory_space=pl.ANY), vmem),
+        in_specs=[vmem] * 2
+        + [pl.BlockSpec(memory_space=pl.ANY)] * 2
+        + [vmem] * 2
+        + [pl.BlockSpec(memory_space=pltpu.SMEM)] * 2,
+        out_specs=(vmem, vmem, pl.BlockSpec(memory_space=pl.ANY), pl.BlockSpec(memory_space=pl.ANY)),
         scratch_shapes=[
+            pltpu.VMEM((4, share, depth), bf16),
+            pltpu.VMEM((8, 128), f32),
+            pltpu.VMEM((lanes, 4 * share), bf16),
             pltpu.VMEM(weight.shape, bf16),
             pltpu.VMEM(ref_weight.shape, bf16),
             pltpu.VMEM((4, 2, 4, count, depth), bf16),
-            pltpu.VMEM((2, ref_rows, ref_depth // 2), f32),
-            pltpu.VMEM((ref_rows, ref_depth // 2), f32),
             pltpu.VMEM((4, 4, 2, 2, 2, 2, 2 * ref_rows, quarter), bf16),
             pltpu.VMEM((4, share, width), f32),
             pltpu.VMEM((4, share, width // 2), i16),
@@ -802,51 +892,41 @@
             pltpu.VMEM((lanes, 128), f32),
             pltpu.VMEM((4, share, 128), f32),
             pltpu.VMEM((4, share, lanes), bf16),
-            pltpu.VMEM((4, lanes, share), bf16),
+            pltpu.VMEM((4, 2 * KEEP, share), bf16),
             pltpu.VMEM((4, 8, lanes), f32),
             pltpu.VMEM((4, share, width), bf16),
-            pltpu.VMEM((lanes, ref_weight.shape[1]), f32),
-            pltpu.VMEM((4, lanes, 128), f32),
+            pltpu.VMEM((4, 4, 2, 2, 2 * ref_rows, ref_weight.shape[1]), f32),
             pltpu.VMEM((4, lanes, 128), f32),
             pltpu.VMEM((4, 8, lanes), f32),
-            pltpu.VMEM((3, 8, lanes), f32),
-            pltpu.VMEM((3, 2, 8, lanes), f32),
-            pltpu.VMEM((7, 2, 8, lanes), f32),
-            pltpu.VMEM((4, 8, lanes), f32),
+            pltpu.VMEM((3, 5, 8, lanes), f32),
+            pltpu.VMEM((7, 5, 8, lanes), f32),
+            pltpu.VMEM((4, 5, 8, lanes), f32),
             pltpu.VMEM((8, lanes), f32),
-            pltpu.VMEM((2, share, width), bf16),
-            pltpu.VMEM((lanes, width), bf16),
+            pltpu.VMEM((2 * KEEP, width), bf16),
             pltpu.VMEM((2, 2, LEN, depth), f32),
             pltpu.VMEM((2, LEN, depth), i16),
-            pltpu.VMEM((4, LEN, depth), i16),
-            pltpu.VMEM((2, LEN, depth), i16),
-            pltpu.VMEM((12, count, depth), i16),
-            pltpu.VMEM((LEN, depth), i16),
             pltpu.VMEM((3, count, depth), i16),
             pltpu.VMEM((LEN, depth), f32),
             pltpu.VMEM((9, 8, lanes), f32),
             pltpu.VMEM((19, 8, lanes), f32),
             pltpu.SemaphoreType.DMA((copies,)),
             pltpu.SemaphoreType.DMA((copies,)),
-            pltpu.SemaphoreType.DMA((6,)),
+            pltpu.SemaphoreType.DMA((12,)),
         ],
         compiler_params=pltpu.CompilerParams(
             collective_id=index, has_side_effects=True, vmem_limit_bytes=VMEM_LIMIT
         ),
-    )(states, others, weight, ref_weight, masks, wanted, pairs)
-
-
-def weight_kernel(states, grad, out, turned):
-    @pl.when(pl.program_id(0) == 0)
-    def _():
-        turned[...] = jnp.transpose(states[...])
-
-    out[...] = jnp.dot(turned[...], grad[...], preferred_element_type=jnp.float32)
-
-
-def weight_gradient(states, grad):
-    tokens, depth = states.shape
-    width = grad.shape[1]
+    )(states, others, weight, ref_weight, masks, wanted, pair_index, chosen)
+
+
+def weight_kernel(turned, grad, out):
+    whole = jnp.concatenate([grad[owner] for owner in range(4)], axis=0)
+    out[...] = jnp.dot(turned[...], whole, preferred_element_type=jnp.float32)
+
+
+def weight_gradient(turned, grad):
+    depth, tokens = turned.shape
+    width = grad.shape[2]
     tile = 512
     return pl.pallas_call(
         weight_kernel,
@@ -854,13 +934,12 @@
         grid=(width // tile,),
         out_shape=jax.ShapeDtypeStruct((depth, width), jnp.float32),
         in_specs=[
-            pl.BlockSpec((tokens, depth), lambda j: (0, 0)),
-            pl.BlockSpec((tokens, tile), lambda j: (0, j)),
+            pl.BlockSpec((depth, tokens), lambda j: (0, 0)),
+            pl.BlockSpec((4, tokens // 4, tile), lambda j: (0, 0, j)),
         ],
         out_specs=pl.BlockSpec((depth, tile), lambda j: (0, j)),
-        scratch_shapes=[pltpu.VMEM((depth, tokens), states.dtype)],
         compiler_params=pltpu.CompilerParams(vmem_limit_bytes=VMEM_LIMIT),
-    )(states, grad)
+    )(turned, grad)
 
 
 def on_device(
@@ -875,18 +954,11 @@
 ):
     masks = response_mask.reshape(4, 1, 2 * LEN)
     wanted = targets.reshape(4, 1, 2 * LEN)
-    sign = (2 * chosen_flag - 1).astype(jnp.float32)
-    same = (pair_index[:, None] == pair_index[None, :]).astype(jnp.float32)
-    pairs = jnp.concatenate(
-        [same * sign[None, :], sign[:, None], jnp.zeros((SEQS, 128 - SEQS - 1), jnp.float32)], axis=1
-    )
 
     def run(index):
         def branch(*operands):
-            loss, grad_states, grad, states = fused(index, SIZES[index], *operands)
-            grad_weight = weight_gradient(
-                states.reshape(-1, states.shape[2]), grad.reshape(-1, grad.shape[2])
-            )
+            loss, grad_states, grad, turned = fused(index, SIZES[index], *operands)
+            grad_weight = weight_gradient(turned, grad.reshape(4, 2 * LEN, -1))
             return (loss[0, 0], grad_states, grad_weight)
 
         return branch
@@ -902,7 +974,8 @@
         reference_weight,
         masks,
         wanted,
-        pairs,
+        pair_index,
+        chosen_flag,
     )
 
 

time: 157 us -> 144 us (0.917)
  Pallas kernels: 151 us -> 139 us
    pallas_call x1, Pallas kernels: 141 us -> 129 us  [fused(): pl.pallas_call(fused_kernel, name='fused_%d' % share, out_shape=(jax.Shap...]
where the time goes in v1:
time: 144 us; the launch traced here: 143 us
  Pallas kernels  139 us (97%)
  local copies, waits for them, and re-layouts  1.87 us (1%)
    pallas_call x1, Pallas kernels, fused(): pl.pallas_call(fused_kernel, name='fused_%d' % share, out_shape=(jax.Shap...  129 us
    pallas_call x1, Pallas kernels, weight_gradient(): pl.pallas_call(weight_kernel, name='weight_gradient', grid=(width // tile...  10.3 us

profile of v1, /device:TPU:0, one launch (start us, length us, event | category | flops | bytes accessed | tf_op | source)
XLA Modules:
  0.0 142.9 jit_solution(6009074810497661063)
XLA Ops:
  0.6 0.7 reshape.21
  1.3 0.1 reduce_sum.9
  1.4 0.6 reduce_max.9
  2.7 139.0 %conditional.1 = (f32[32,1280]{1,0:T(8,128)S(1)}, f32[1280,2560]{1,0:T(8,128)}, f32[8,128]{1,0:T(8,128)S(1)}) conditional(s32[]{:T(128)} %clamp.3, (bf16[32,1280]{1,0:T(8,128)(2,1)}, bf16[8,5120]{1,0:T(8,128)(2,1)}, bf16[1280,2560]{1,0:T(8,128)(2,1)}, bf16[5120,640]{1,0:T(8,128)(2,1)}, s32[1024]{0:T(1024)}, /*index=5*/s32[1024]{0:T(1024)}, ...), branch_computations={%region_2.0_spmd, %region_3.0_spmd} | conditional | bytes 24 | solution.py:968
  2.7 128.7 %fused_176.1 = (f32[8,128]{1,0:T(8,128)S(1)}, f32[32,1280]{1,0:T(8,128)S(1)}, bf16[4,4,2,2,16,2560]{5,4,3,2,1,0:T(8,128)(2,1)}, bf16[1280,704]{1,0:T(8,128)(2,1)}) custom-call(bf16[32,1280]{1,0:T(8,128)(2,1)} %get-tuple-element.77.own, bf16[8,5120]{1,0:T(8,128)(2,1)} %get-tuple-element.79.ref_own, bf16[1280,2560]{1,0:T(8,128)(2,1)} %get-tuple-element.81.weight_in, ...), custom_call_target="tpu_custom_call" | custom-call | tf_op jit(solution)/shard_map/cond/branch_0_fun/fused_176/pallas_call | solution.py:863
  131.4 10.3 %weight_gradient.2 = f32[1280,2560]{1,0:T(8,128)} custom-call(bf16[1280,704]{1,0:T(8,128)(2,1)} %get-tuple-element.42.turned, bf16[4,256,2560]{2,1,0:T(8,128)(2,1)} %bitcast.8), custom_call_target="tpu_custom_call" | custom-call | tf_op jit(solution)/shard_map/cond/branch_0_fun/weight_gradient/pallas_call | solution.py:931
  141.7 0.5 slice.6
  142.2 0.7 copy.36
